TPU v7x, 32 devices: a whole 2x2x4 slice. The times are simulated.
32 devices in a mesh: groups: 2 (over x), vocab: 8 (over z, y), rows: 2 (over core).
Axes of the slice: x: 2, y: 2, z: 4, core: 2. Of those that a mesh axis runs over, the one named last changes fastest.
Arguments:
- teacher_hidden: bfloat16 [256, 4608], P(('groups', 'vocab', 'rows')), parts along dimension 0, may hold values from -24 to 24
- student_hidden: bfloat16 [256, 3584], P(('groups', 'vocab', 'rows')), parts along dimension 0, may hold values from -24 to 24
- teacher_head: bfloat16 [4608, 5120], P(None, 'vocab'), may hold values from -0.09375 to 0.09375
- student_head: bfloat16 [3584, 5120], P(None, 'vocab'), may hold values from -0.09375 to 0.09375
- dest_slot: int32 [256], P(('groups', 'vocab', 'rows')), parts along dimension 0, may hold values from 0 to 15, as said below
- targets: int32 [256], P(('groups', 'vocab', 'rows')), parts along dimension 0, may hold values from 0 to 5119
- token_grad: bfloat16 [256], P(('groups', 'vocab', 'rows')), parts along dimension 0, may hold values from 50 to 500
Outputs:
- token_loss: float32 [256], P(('groups', 'vocab', 'rows')), parts along dimension 0
- hidden_grad: bfloat16 [256, 3584], P(('groups', 'vocab', 'rows')), parts along dimension 0
There are 2 independent parts, one for each index of `groups`. A program takes and returns all parts, laid end to end along the dimension named above; an argument that names none is the same for every part. Nothing has to cross between parts.
Inputs may be any that keep to these rules, and one draw needn't show every extreme that they name: Within each pair block of 16 consecutive rows, dest_slot is a permutation of 0 to 15.
All inputs are finite; a program needn't handle non-finite values.
Results may differ from a plain program's by a relative error of at most 0.0048.
Values may be sent and summed in bfloat16 or wider, within the bound.
A program may use at most 64 MiB of HBM per device.

v0:
```python
import jax
import jax.numpy as jnp
from jax import lax
from jax.sharding import PartitionSpec as P

soft_cap = 30.0


def capped(values):
    return soft_cap * jnp.tanh(values / soft_cap)


def local(
    teacher_hidden, student_hidden, teacher_head, student_head, dest_slot, targets, token_grad
):
    local_rows = student_hidden.shape[0]
    width_t = teacher_hidden.shape[1]
    shard_voc = student_head.shape[1]
    row_count = lax.axis_size("rows")
    vocab_index = lax.axis_index("vocab")
    packed = (
        jnp.zeros((row_count * local_rows, width_t), jnp.bfloat16).at[dest_slot].set(teacher_hidden)
    )
    arrived = lax.all_to_all(
        packed.reshape(row_count, local_rows, width_t),
        "rows",
        split_axis=0,
        concat_axis=0,
        tiled=True,
    )
    aligned = arrived[0]
    aligned = aligned + arrived[1]
    teacher_group = lax.all_gather(aligned, "vocab", axis=0, tiled=True)
    student_group, target_group, weight_group = (
        lax.all_gather(student_hidden, "vocab", axis=0, tiled=True),
        lax.all_gather(targets, "vocab", axis=0, tiled=True),
        lax.all_gather(token_grad, "vocab", axis=0, tiled=True),
    )
    columns = vocab_index * shard_voc + jnp.arange(shard_voc, dtype=jnp.int32)
    onehot = target_group[:, None] == columns[None, :]
    logit_t = capped(jnp.dot(teacher_group, teacher_head, preferred_element_type=jnp.float32))
    exp_t = jnp.exp(logit_t)
    logit_s = capped(jnp.dot(student_group, student_head, preferred_element_type=jnp.float32))
    exp_s = jnp.exp(logit_s)
    norm_t, cross, norm_s, hit = lax.psum(
        (
            jnp.sum(exp_t, axis=1),
            jnp.sum(exp_t * (logit_t - logit_s), axis=1),
            jnp.sum(exp_s, axis=1),
            jnp.sum(jnp.where(onehot, logit_s, 0.0), axis=1),
        ),
        "vocab",
    )
    loss_group = cross / norm_t - jnp.log(norm_t) + 2.0 * jnp.log(norm_s) - hit
    token_loss = lax.dynamic_slice_in_dim(loss_group, vocab_index * local_rows, local_rows, 0)
    slope = 1.0 - logit_s / soft_cap * (logit_s / soft_cap)
    grad = (
        weight_group.astype(jnp.float32)[:, None]
        * (2.0 * exp_s / norm_s[:, None] - exp_t / norm_t[:, None] - onehot.astype(jnp.float32))
        * slope
    )
    grad = grad.astype(jnp.bfloat16)
    hidden_grad = lax.psum_scatter(
        lax.dot_general(
            grad, student_head, (((1,), (1,)), ((), ())), preferred_element_type=jnp.float32
        ),
        "vocab",
        scatter_dimension=0,
        tiled=True,
    ).astype(jnp.bfloat16)
    return (token_loss, hidden_grad)


def solution(mesh):
    placed = (
        P(("groups", "vocab", "rows"), None),
        P(("groups", "vocab", "rows"), None),
        P(None, "vocab"),
        P(None, "vocab"),
        P(("groups", "vocab", "rows")),
        P(("groups", "vocab", "rows")),
        P(("groups", "vocab", "rows")),
    )
    return jax.shard_map(
        local,
        mesh=mesh,
        in_specs=placed,
        out_specs=(P(("groups", "vocab", "rows")), P(("groups", "vocab", "rows"), None)),
        check_vma=False,
    )
```

profile of v0, /device:TPU:0, one launch (start us, length us, event | category | flops | bytes accessed | tf_op | source)
XLA Modules:
  0.0 209.5 jit_solution(5858274301826109229)
XLA Ops:
  7.2 0.7 compare_select_fusion.1
  7.8 1.7 scatter_custom_fusion
  9.5 3.4 %all-to-all-start = ((bf16[2,8,4608]{2,1,0:T(8,128)(2,1)}), bf16[2,8,4608]{2,1,0:T(8,128)(2,1)S(1)}, u32[]{:S(2)}, u32[]{:S(2)}) async-start(bf16[2,8,4608]{2,1,0:T(8,128)(2,1)} %bitcast), calls=%async_computation | async-start | bytes 294912 | tf_op jit(solution)/shard_map/all_to_all | solution.py:24
  12.9 0.0 reduce-scatter.2.cloned.1.call-start
  13.0 1.2 dynamic-slice
  14.9 0.9 dynamic-update-slice.1
  15.8 23.1 %all-reduce.1 = bf16[64]{0:T(256)(128)(2,1)S(1)} all-reduce(bf16[64]{0:T(256)(128)(2,1)S(1)} %dynamic-update-slice.1), channel_id=1, replica_groups=mesh['groups'=2,'vocab'=8,'rows'=2] {'vocab'}, use_global_device_ids=true, to_apply=%add.1 | all-reduce | flops 64 | bytes 256
  38.9 0.9 dynamic-update-slice
  39.7 6.8 %all-reduce = s32[64]{0:T(128)S(1)} all-reduce(s32[64]{0:T(128)S(1)} %dynamic-update-slice), channel_id=1, replica_groups=mesh['groups'=2,'vocab'=8,'rows'=2] {'vocab'}, use_global_device_ids=true, to_apply=%add | all-reduce | flops 64 | bytes 512
  46.5 33.2 %all_gather.13 = bf16[64,3584]{1,0:T(8,128)(2,1)S(1)} all-gather(bf16[8,3584]{1,0:T(8,128)(2,1)} %param.8), channel_id=1, replica_groups=mesh['groups'=2,'vocab'=8,'rows'=2] {'vocab'}, dimensions={0}, use_global_device_ids=true | all-gather | bytes 516096 | tf_op jit(solution)/shard_map/all_gather | solution.py:35
  79.7 0.0 all-to-all-done
  79.7 0.0 copy-start
  79.7 31.6 %all-gather = bf16[1,64,4608]{2,1,0:T(8,128)(2,1)S(1)} all-gather(bf16[1,8,4608]{2,1,0:T(8,128)(2,1)S(1)} %slice_add_fusion), channel_id=2, replica_groups=mesh['groups'=2,'vocab'=8,'rows'=2] {'vocab'}, dimensions={1}, use_global_device_ids=true | all-gather | bytes 663552 | tf_op jit(solution)/shard_map/all_gather | solution.py:33
  111.3 3.2 %fusion = f32[64,640]{1,0:T(8,128)S(1)} fusion(bf16[64,3584]{1,0:T(8,128)(2,1)S(1)} %all_gather.13, bf16[3584,640]{1,0:T(8,128)(2,1)} %param.10), kind=kOutput, calls=%fused_computation.2 | convolution fusion | flops 293642240 | bytes 5210112 | tf_op jit(solution)/shard_map/dot_general | solution.py:43
  114.5 0.0 copy-done
  114.5 1.3 multiply_reduce_fusion
  115.8 19.8 %all-reduce.2 = (f32[64]{0:T(128)S(1)}, f32[64]{0:T(128)S(1)}, f32[64]{0:T(128)S(1)}, f32[64]{0:T(128)S(1)}) all-reduce(f32[64]{0:T(128)S(1)} %get-tuple-element.4, f32[64]{0:T(128)S(1)} %get-tuple-element.3, f32[64]{0:T(128)S(1)} %get-tuple-element.5, ...), channel_id=1, replica_groups=mesh['groups'=2,'vocab'=8,'rows'=2] {'vocab'}, use_global_device_ids=true, to_apply=%region_8.9 | all-reduce | flops 256 | bytes 2048 | tf_op jit(solution)/shard_map/psum | solution.py:45
  135.6 4.8 %fusion.9 = f32[64,3584]{1,0:T(8,128)} fusion(bf16[3584,640]{1,0:T(8,128)(2,1)} %param.10, f32[64,640]{1,0:T(8,128)S(1)} %fusion, f32[64,640]{1,0:T(8,128)S(1)} %get-tuple-element.10, f32[64]{0:T(128)S(1)} %get-tuple-element.8, f32[64]{0:T(128)S(1)} %get-tuple-element.7, f32[64]{0:T(128)S(1)} %convert_element_type.12, s32[640]{0:T(1024)S(1)} %iota_add_fusion, ...), kind=kOutput, calls=%fused_computation.17 | convolution fusion | flops 294133760 | bytes 5836288 | tf_op jit(solution)/shard_map/dot_general | solution.py:64
  140.3 0.0 reduce-scatter.2.cloned.1.call-update
  140.4 0.6 dynamic_slice.3
  141.0 60.1 %reduce-scatter.2.cloned.1.call-done = f32[8,3584]{1,0:T(8,128)} async-done(((f32[64,3584]{1,0:T(8,128)}), f32[8,3584]{1,0:T(8,128)}) %reduce-scatter.2.cloned.1.call-update) | async-done | bytes 114704 | tf_op jit(solution)/shard_map/reduce_scatter | solution.py:63
  201.1 1.5 convert_element_type.15
  (6 shorter events, 0.0 us)
Async XLA Ops:
  9.5 70.2 %all-to-all-start = ((bf16[2,8,4608]{2,1,0:T(8,128)(2,1)}), bf16[2,8,4608]{2,1,0:T(8,128)(2,1)S(1)}, u32[]{:S(2)}, u32[]{:S(2)}) async-start(bf16[2,8,4608]{2,1,0:T(8,128)(2,1)} %bitcast), calls=%async_computation | async-start | bytes 294912 | tf_op jit(solution)/shard_map/all_to_all | solution.py:24
  12.9 188.2 %reduce-scatter.2.cloned.1.call-start = ((), (), s32[]{:S(2)}) async-start(), calls=%async_computation.2 | async-start | bytes 1032192 | tf_op jit(solution)/shard_map/reduce_scatter | solution.py:63
  79.7 34.8 %copy-start = (bf16[4608,640]{1,0:T(8,128)(2,1)S(1)}, bf16[4608,640]{1,0:T(8,128)(2,1)}, u32[]{:S(2)}) copy-start(bf16[4608,640]{1,0:T(8,128)(2,1)} %param.9) | copy-start | bytes 17694724
Sparse Core Ops, SparseCore 0:
  140.5 60.5 reduce-scatter.1
where the time goes:
time: 210 us; the launch traced here: 209 us
  blocking collectives  114 us (54%)
  waiting for transfers between devices  60.1 us (29%)
  between operations  14.7 us (7%)
  matrix products  9.25 us (4%)
  local copies, waits for them, and re-layouts  5.23 us (2%)
  starting transfers between devices  3.46 us (2%)
  other arithmetic  2.22 us (1%)
    reduce_scatter x1, waiting for transfers between devices, local(): lax.psum_scatter(lax.dot_general(grad, student_head, (((1,), (1,)), ((),...  60.1 us
    all_gather x1, blocking collectives, local(): lax.all_gather(student_hidden, 'vocab', axis=0, tiled=True)  33.2 us
    all_gather x1, blocking collectives, local(): teacher_group = lax.all_gather(aligned, 'vocab', axis=0, tiled=True)  31.6 us
    unnamed x2, blocking collectives  29.9 us
    psum x1, blocking collectives, local(): lax.psum((jnp.sum(exp_t, axis=1), jnp.sum(exp_t * (logit_t - logit_s), ax...  19.8 us
    dot_general x1, matrix products, local(): lax.dot_general(grad, student_head, (((1,), (1,)), ((), ())), preferred_e...  4.77 us
  transfers between devices with their start and end apart: 2, of which 1 were waited for; matrix products, arithmetic and copies ran while one was open for 2% of the time, Pallas kernels for 0%

commit v1 on v0

v1 whole, which is shorter than its diff:
```python
import functools

import jax
import jax.numpy as jnp
from jax import lax
from jax.experimental import pallas as pl
from jax.experimental.pallas import tpu as pltpu
from jax.sharding import PartitionSpec as P

soft_cap = 30.0
CHUNKS = 4
BACK = 2
F32 = jnp.float32
BF16 = jnp.bfloat16


def capped(values):
    return soft_cap * jnp.tanh(values / soft_cap)


def iota(shape, dim):
    return lax.broadcasted_iota(jnp.int32, shape, dim)


def to_row(column):
    size = column.shape[0]
    eye = iota((size, size), 0) == iota((size, size), 1)
    return jnp.sum(jnp.where(eye, column, 0.0), axis=0, keepdims=True)


def to_column(row):
    size = row.shape[1]
    eye = iota((size, size), 0) == iota((size, size), 1)
    return jnp.sum(jnp.where(eye, row, 0.0), axis=1, keepdims=True)


def stacked(values):
    half = values.shape[1] // 2
    return jnp.concatenate([values[:, :half], values[:, half:]], axis=0)


def kernel(
    far, near,
    th_ref, sh_ref, dest_ref, target_ref, weight_ref, thead_ref, shead_ref,
    loss_ref, hidden_ref,
    heads, swap_out, swap_in, blocks, meta, stats, lt, ls, back_out, back_in,
    head_sem, swap_sem, arrive, up_sem, down_sem, side_sem,
    meta_send, meta_recv, stat_send, stat_recv, back_send, back_recv,
):
    n = far * near
    rows, wide_t = th_ref.shape
    wide_s = sh_ref.shape[1]
    half = (wide_t + wide_s) // 2
    chunk = half // CHUNKS
    shard = heads.shape[1]
    tokens = n * rows
    v = lax.axis_index("vocab")
    r = lax.axis_index("rows")
    z, y = lax.div(v, near), lax.rem(v, near)

    loads = [
        pltpu.make_async_copy(thead_ref, heads.at[pl.ds(0, wide_t)], head_sem.at[0]),
        pltpu.make_async_copy(shead_ref, heads.at[pl.ds(wide_t, wide_s)], head_sem.at[1]),
    ]
    for load in loads:
        load.start()

    barrier = pltpu.get_barrier_semaphore()
    pl.semaphore_signal(barrier, inc=1, device_id={"rows": 1 - r})
    for step in range(1, n):
        pl.semaphore_signal(barrier, inc=1, device_id={"vocab": lax.rem(v + step, n)})

    lanes = iota((rows, rows), 1)
    place = iota((rows, rows), 0)
    slots = jnp.zeros((rows, rows), jnp.int32)
    for j in range(rows):
        slots = jnp.where(lanes == j, dest_ref[j], slots)
    teacher = th_ref[...]

    def picked(core):
        chosen = jnp.where(slots == core * rows + place, 1.0, 0.0).astype(BF16)
        return jnp.dot(chosen, teacher, preferred_element_type=F32)

    swap_out[...] = stacked(picked(1 - r)).astype(BF16)
    row_at = iota((rows, 128), 0)
    lane_at = iota((rows, 128), 1)
    own_meta = jnp.where(
        lane_at == 1, to_column(weight_ref[...].astype(F32).reshape(1, rows)), 0.0
    )
    for j in range(rows):
        own_meta = jnp.where((lane_at == 0) & (row_at == j), target_ref[j].astype(F32), own_meta)
    meta[v] = own_meta
    kept = picked(r)
    pl.semaphore_wait(barrier, n)

    swap = pltpu.make_async_remote_copy(
        swap_out, swap_in, swap_sem.at[0], swap_sem.at[1], device_id={"rows": 1 - r}
    )
    swap.start()

    def to_all(src, dst, sends, recvs):
        copies = []
        for step in range(1, n):
            copies.append(
                pltpu.make_async_remote_copy(
                    src, dst, sends.at[step - 1], recvs.at[step - 1],
                    device_id={"vocab": lax.rem(v + step, n)},
                )
            )
            copies[-1].start()
        return copies

    meta_copies = to_all(meta.at[v], meta.at[v], meta_send, meta_recv)
    swap.wait_recv()
    moved = swap_in[...].astype(F32)
    aligned = kept + jnp.concatenate([moved[:rows], moved[rows:]], axis=1)
    own = stacked(jnp.concatenate([aligned, sh_ref[...].astype(F32)], axis=1))
    blocks[v] = own.astype(BF16)

    def piece(source, c):
        return blocks.at[source, :, pl.ds(c * chunk, chunk)]

    def vertical(source, c, up):
        source_z = lax.div(source, near)
        sems = up_sem if up else down_sem
        return pltpu.make_async_remote_copy(
            piece(source, c), piece(source, c), sems.at[source_z, c], arrive.at[source, c],
            device_id={"vocab": v + near if up else v - near},
        )

    def sideways(source, c, step):
        source_z = lax.div(source, near)
        return pltpu.make_async_remote_copy(
            piece(source, c), piece(source, c), side_sem.at[step - 1, source_z, c],
            arrive.at[source, c],
            device_id={"vocab": z * near + lax.rem(y + step, near)},
        )

    def spread(source, c, up, down):
        if up:
            @pl.when(z < far - 1)
            def _():
                vertical(source, c, True).start()
        if down:
            @pl.when(z > 0)
            def _():
                vertical(source, c, False).start()
        for step in range(1, near):
            sideways(source, c, step).start()

    def product(c):
        both = blocks[:, :, c * chunk:(c + 1) * chunk].astype(F32)
        for part in range(2):
            x = both[:, part * rows:(part + 1) * rows].reshape(tokens, chunk).astype(BF16)
            first = part * half + c * chunk
            for out, begin, end in ((lt, 0, wide_t), (ls, wide_t, wide_t + wide_s)):
                low, high = max(first, begin), min(first + chunk, end)
                if low < high:
                    out[...] += jnp.dot(
                        x[:, low - first:high - first], heads[low:high, :],
                        preferred_element_type=F32,
                    )

    lt[...] = jnp.zeros_like(lt)
    ls[...] = jnp.zeros_like(ls)
    spread(v, 0, True, True)
    for t in range(CHUNKS + far):
        if t + 1 < CHUNKS:
            spread(v, t + 1, True, True)
        for d in range(1, far):
            c = t - d
            if 0 <= c < CHUNKS:
                @pl.when(z >= d)
                def _():
                    vertical(v - d * near, c, True).wait_recv()
                    spread(v - d * near, c, True, False)

                @pl.when(z + d < far)
                def _():
                    vertical(v + d * near, c, False).wait_recv()
                    spread(v + d * near, c, False, True)
        c = t - far
        if c >= 0:
            for step in range(1, near):
                for source_z in range(far):
                    source = source_z * near + lax.rem(y + step, near)
                    sideways(source, c, step).wait_recv()
            if c == 0:
                for load in loads:
                    load.wait()
            product(c)
    for copy in meta_copies:
        copy.wait_recv()

    info = meta[...].reshape(tokens, 128)
    target = info[:, 0:1].astype(jnp.int32) - v * shard
    weight = info[:, 1:2]
    onehot = iota((tokens, shard), 1) == target
    logit_t = capped(lt[...])
    exp_t = jnp.exp(logit_t)
    logit_s = capped(ls[...])
    exp_s = jnp.exp(logit_s)
    sums = (
        jnp.sum(exp_t, axis=1, keepdims=True),
        jnp.sum(exp_t * (logit_t - logit_s), axis=1, keepdims=True),
        jnp.sum(exp_s, axis=1, keepdims=True),
        jnp.sum(jnp.where(onehot, logit_s, 0.0), axis=1, keepdims=True),
    )
    stat_row = iota((8, tokens), 0)
    mine = jnp.zeros((8, tokens), F32)
    for k, column in enumerate(sums):
        mine = jnp.where(stat_row == k, to_row(column), mine)
    stats[v] = mine
    stat_copies = to_all(stats.at[v], stats.at[v], stat_send, stat_recv)
    slope = 1.0 - (logit_s / soft_cap) * (logit_s / soft_cap)
    for copy in stat_copies:
        copy.wait_recv()
    total = jnp.sum(stats[...], axis=0)
    norm_t, cross, norm_s, hit = (total[k:k + 1] for k in range(4))
    zt, zs = to_column(norm_t), to_column(norm_s)
    grad = (
        weight
        * (exp_s * (2.0 / zs) - exp_t * (1.0 / zt) - jnp.where(onehot, 1.0, 0.0))
        * slope
    ).astype(BF16)

    cols = wide_s // 2 // BACK

    def backed(q, part):
        first = wide_t + part * (wide_s // 2) + q * cols
        return lax.dot_general(
            grad, heads[first:first + cols, :], (((1,), (1,)), ((), ())),
            preferred_element_type=F32,
        ).astype(BF16).astype(F32).reshape(n, rows, cols)

    back_copies = []
    for q in range(BACK):
        joined = jnp.concatenate([backed(q, 0), backed(q, 1)], axis=1)
        back_out[:, q] = joined.astype(BF16)
        for step in range(1, n):
            there = lax.rem(v + step, n)
            back_copies.append(
                pltpu.make_async_remote_copy(
                    back_out.at[there, q], back_in.at[step - 1, q],
                    back_send.at[step - 1, q], back_recv.at[step - 1, q],
                    device_id={"vocab": there},
                )
            )
            back_copies[-1].start()

    loss = cross / norm_t - jnp.log(norm_t) + 2.0 * jnp.log(norm_s) - hit
    choose = iota((rows, tokens), 1) == v * rows + iota((rows, tokens), 0)
    loss_ref[...] = to_row(jnp.sum(jnp.where(choose, loss, 0.0), axis=1, keepdims=True))

    k = 0
    for q in range(BACK):
        result = back_out[v, q].astype(F32)
        for step in range(1, n):
            back_copies[k].wait_recv()
            k += 1
            result += back_in[step - 1, q].astype(F32)
        result = jnp.concatenate([result[:rows], result[rows:]], axis=1).astype(BF16)
        hidden_ref[:, q * cols:(q + 1) * cols] = result[:, :cols]
        hidden_ref[:, wide_s // 2 + q * cols:wide_s // 2 + (q + 1) * cols] = result[:, cols:]

    swap.wait_send()
    for copy in meta_copies + stat_copies + back_copies:
        copy.wait_send()
    for c in range(CHUNKS):
        for d in range(far):
            @pl.when((z >= d) & (z < far - 1))
            def _():
                vertical(v - d * near, c, True).wait_send()

            @pl.when((z + d < far) & (z > 0))
            def _():
                vertical(v + d * near, c, False).wait_send()
        for source_z in range(far):
            for step in range(1, near):
                sideways(source_z * near + y, c, step).wait_send()


def local(far, near, teacher_hidden, student_hidden, teacher_head, student_head, dest_slot, targets, token_grad):
    n = far * near
    rows, wide_t = teacher_hidden.shape
    wide_s = student_hidden.shape[1]
    shard = student_head.shape[1]
    tokens = n * rows
    half = (wide_t + wide_s) // 2
    vmem = pl.BlockSpec(memory_space=pltpu.VMEM)
    smem = pl.BlockSpec(memory_space=pltpu.SMEM)
    hbm = pl.BlockSpec(memory_space=pl.ANY)
    dma = pltpu.SemaphoreType.DMA
    loss, hidden = pl.pallas_call(
        functools.partial(kernel, far, near),
        out_shape=(
            jax.ShapeDtypeStruct((1, rows), F32),
            jax.ShapeDtypeStruct((rows, wide_s), BF16),
        ),
        in_specs=[vmem, vmem, smem, smem, vmem, hbm, hbm],
        out_specs=(vmem, vmem),
        scratch_shapes=[
            pltpu.VMEM((wide_t + wide_s, shard), BF16),
            pltpu.VMEM((2 * rows, wide_t // 2), BF16),
            pltpu.VMEM((2 * rows, wide_t // 2), BF16),
            pltpu.VMEM((n, 2 * rows, half), BF16),
            pltpu.VMEM((n, rows, 128), F32),
            pltpu.VMEM((n, 8, tokens), F32),
            pltpu.VMEM((tokens, shard), F32),
            pltpu.VMEM((tokens, shard), F32),
            pltpu.VMEM((n, BACK, 2 * rows, wide_s // 2 // BACK), BF16),
            pltpu.VMEM((n - 1, BACK, 2 * rows, wide_s // 2 // BACK), BF16),
            dma((2,)),
            dma((2,)),
            dma((n, CHUNKS)),
            dma((far, CHUNKS)),
            dma((far, CHUNKS)),
            dma((near - 1, far, CHUNKS)),
            dma((n - 1,)),
            dma((n - 1,)),
            dma((n - 1,)),
            dma((n - 1,)),
            dma((n - 1, BACK)),
            dma((n - 1, BACK)),
        ],
        compiler_params=pltpu.CompilerParams(
            collective_id=0, has_side_effects=True, vmem_limit_bytes=56 * 2**20
        ),
    )(teacher_hidden, student_hidden, dest_slot, targets, token_grad, teacher_head, student_head)
    return loss.reshape(rows), hidden


def solution(mesh):
    n = mesh.shape["vocab"]
    near = 1 << ((n.bit_length() - 1) // 2)
    far = n // near
    by_token = P(("groups", "vocab", "rows"))
    by_row = P(("groups", "vocab", "rows"), None)
    by_vocab = P(None, "vocab")
    return jax.shard_map(
        functools.partial(local, far, near),
        mesh=mesh,
        in_specs=(by_row, by_row, by_vocab, by_vocab, by_token, by_token, by_token),
        out_specs=(by_token, by_row),
        check_vma=False,
    )
```

time: 210 us -> 44.5 us (0.21)
  blocking collectives: 114 us -> 0 us
  waiting for transfers between devices: 60.1 us -> 0 us
  Pallas kernels: 0 us -> 41.1 us
  between operations: 14.7 us -> 0.64 us
  matrix products: 9.25 us -> 0 us
  starting transfers between devices: 3.46 us -> 0 us
  local copies, waits for them, and re-layouts: 5.23 us -> 2.56 us
  other arithmetic: 2.22 us -> 0 us
    all_gather x2 -> x0, blocking collectives: 64.8 us -> none  [the longest x1 33.2 us: local(): lax.all_gather(student_hidden, 'vocab', axis=0, tiled=True)]
    reduce_scatter x1 -> x0, waiting for transfers between devices: 60.1 us -> none  [local(): lax.psum_scatter(lax.dot_general(grad, student_head, (((1,), (1,)), ((),...]
    pallas_call x0 -> x1, Pallas kernels: none -> 41.1 us  [local(): pl.pallas_call(functools.partial(kernel, far, near), out_shape=(jax.Shape...]
    unnamed x2 -> x0, blocking collectives: 29.9 us -> none
    psum x1 -> x0, blocking collectives: 19.8 us -> none  [local(): lax.psum((jnp.sum(exp_t, axis=1), jnp.sum(exp_t * (logit_t - logit_s), ax...]
    dot_general x3 -> x0, matrix products: 9.25 us -> none  [the longest x1 4.77 us: local(): lax.dot_general(grad, student_head, (((1,), (1,)), ((), ())), preferred_e...]
    all_to_all x1 -> x0, starting transfers between devices: 3.42 us -> none  [local(): lax.all_to_all(packed.reshape(row_count, local_rows, width_t), 'rows', sp...]
  transfers between devices with their start and end apart: 2 -> 0, of which waited for: 1 -> 0; matrix products, arithmetic and copies ran while one was open for 2% -> 0% of each run, Pallas kernels for 0% -> 0%
where the time goes in v1:
time: 44.5 us; the launch traced here: 44.3 us
  Pallas kernels  41.1 us (92%)
  local copies, waits for them, and re-layouts  2.56 us (6%)
  between operations  0.64 us (1%)
    pallas_call x1, Pallas kernels, local(): pl.pallas_call(functools.partial(kernel, far, near), out_shape=(jax.Shape...  41.1 us
    unnamed x2, local copies, waits for them, and re-layouts  2.56 us

profile of v1, /device:TPU:0, one launch (start us, length us, event | category | flops | bytes accessed | tf_op | source)
XLA Modules:
  0.0 44.3 jit_solution(5666309785037492968)
XLA Ops:
  0.6 41.1 %shard_map.86 = (f32[1,8]{1,0:T(1,128)}, bf16[8,3584]{1,0:T(8,128)(2,1)}) custom-call(bf16[8,4608]{1,0:T(8,128)(2,1)} %th_ref.1, bf16[8,3584]{1,0:T(8,128)(2,1)} %sh_ref.1, s32[8]{0:T(128)} %dest_ref.1, s32[8]{0:T(128)} %target_ref.1, bf16[8]{0:T(256)(128)(2,1)} %weight_ref.1, bf16[4608,640]{1,0:T(8,128)(2,1)} %thead_ref.1, bf16[3584,640]{1,0:T(8,128)(2,1)} %shead_ref.1), custom_call_target="tpu_custom_call" | custom-call | tf_op jit(solution)/shard_map/pallas_call | solution.py:294
  41.7 1.1 %copy.11 = f32[8]{0:T(128)} copy(f32[8]{0:T(128)} %bitcast.1) | data formatting | bytes 64
  42.9 1.4 %copy.12 = bf16[8,3584]{1,0:T(8,128)(2,1)} copy(bf16[8,3584]{1,0:T(8,128)(2,1)} %get-tuple-element.9) | data formatting | bytes 114688

commit v2 on v1

--- a/solution.py
+++ b/solution.py
@@ -8,8 +8,8 @@
 from jax.sharding import PartitionSpec as P
 
 soft_cap = 30.0
-CHUNKS = 4
-BACK = 2
+CHUNKS = 2
+BACK = 1
 F32 = jnp.float32
 BF16 = jnp.bfloat16
 
@@ -41,11 +41,11 @@
 
 def kernel(
     far, near,
-    th_ref, sh_ref, dest_ref, target_ref, weight_ref, thead_ref, shead_ref,
+    th_in, sh_in, dest_in, target_in, weight_ref, thead_ref, shead_ref,
     loss_ref, hidden_ref,
-    heads, swap_out, swap_in, blocks, meta, stats, lt, ls, back_out, back_in,
-    head_sem, swap_sem, arrive, up_sem, down_sem, side_sem,
-    meta_send, meta_recv, stat_send, stat_recv, back_send, back_recv,
+    th_ref, sh_ref, dest_ref, target_ref, heads, swap_out, swap_in, blocks, stats, lt, ls, back_out, back_in,
+    small_sem, head_sem, swap_sem, arrive, up_sem, down_sem, side_sem,
+    stat_send, stat_recv, back_send, back_recv,
 ):
     n = far * near
     rows, wide_t = th_ref.shape
@@ -58,6 +58,19 @@
     r = lax.axis_index("rows")
     z, y = lax.div(v, near), lax.rem(v, near)
 
+    barrier = pltpu.get_barrier_semaphore()
+    pl.semaphore_signal(barrier, inc=1, device_id={"rows": 1 - r})
+    for step in range(1, n):
+        pl.semaphore_signal(barrier, inc=1, device_id={"vocab": lax.rem(v + step, n)})
+
+    small = [
+        pltpu.make_async_copy(src, dst, small_sem.at[at])
+        for at, (src, dst) in enumerate(
+            ((th_in, th_ref), (dest_in, dest_ref), (target_in, target_ref), (sh_in, sh_ref))
+        )
+    ]
+    for load in small:
+        load.start()
     loads = [
         pltpu.make_async_copy(thead_ref, heads.at[pl.ds(0, wide_t)], head_sem.at[0]),
         pltpu.make_async_copy(shead_ref, heads.at[pl.ds(wide_t, wide_s)], head_sem.at[1]),
@@ -65,10 +78,8 @@
     for load in loads:
         load.start()
 
-    barrier = pltpu.get_barrier_semaphore()
-    pl.semaphore_signal(barrier, inc=1, device_id={"rows": 1 - r})
-    for step in range(1, n):
-        pl.semaphore_signal(barrier, inc=1, device_id={"vocab": lax.rem(v + step, n)})
+    for load in small:
+        load.wait()
 
     lanes = iota((rows, rows), 1)
     place = iota((rows, rows), 0)
@@ -85,11 +96,15 @@
     row_at = iota((rows, 128), 0)
     lane_at = iota((rows, 128), 1)
     own_meta = jnp.where(
-        lane_at == 1, to_column(weight_ref[...].astype(F32).reshape(1, rows)), 0.0
+        lane_at == 2, to_column(weight_ref[...].astype(F32).reshape(1, rows)), 0.0
     )
     for j in range(rows):
-        own_meta = jnp.where((lane_at == 0) & (row_at == j), target_ref[j].astype(F32), own_meta)
-    meta[v] = own_meta
+        own_meta = jnp.where(
+            (row_at == j) & (lane_at == 0), lax.div(target_ref[j], 256).astype(F32),
+            jnp.where(
+                (row_at == j) & (lane_at == 1), lax.rem(target_ref[j], 256).astype(F32), own_meta
+            ),
+        )
     kept = picked(r)
     pl.semaphore_wait(barrier, n)
 
@@ -110,15 +125,15 @@
             copies[-1].start()
         return copies
 
-    meta_copies = to_all(meta.at[v], meta.at[v], meta_send, meta_recv)
     swap.wait_recv()
     moved = swap_in[...].astype(F32)
     aligned = kept + jnp.concatenate([moved[:rows], moved[rows:]], axis=1)
     own = stacked(jnp.concatenate([aligned, sh_ref[...].astype(F32)], axis=1))
-    blocks[v] = own.astype(BF16)
+    blocks[v, :, :half] = own.astype(BF16)
+    blocks[v, :, half:] = jnp.concatenate([own_meta, jnp.zeros_like(own_meta)], axis=0).astype(BF16)
 
     def piece(source, c):
-        return blocks.at[source, :, pl.ds(c * chunk, chunk)]
+        return blocks.at[source, :, pl.ds(c * chunk, chunk + 128 if c == CHUNKS - 1 else chunk)]
 
     def vertical(source, c, up):
         source_z = lax.div(source, near)
@@ -165,8 +180,9 @@
     ls[...] = jnp.zeros_like(ls)
     spread(v, 0, True, True)
     for t in range(CHUNKS + far):
-        if t + 1 < CHUNKS:
-            spread(v, t + 1, True, True)
+        if t == 0:
+            for c in range(1, CHUNKS):
+                spread(v, c, True, True)
         for d in range(1, far):
             c = t - d
             if 0 <= c < CHUNKS:
@@ -189,12 +205,10 @@
                 for load in loads:
                     load.wait()
             product(c)
-    for copy in meta_copies:
-        copy.wait_recv()
-
-    info = meta[...].reshape(tokens, 128)
-    target = info[:, 0:1].astype(jnp.int32) - v * shard
-    weight = info[:, 1:2]
+
+    info = blocks[:, :, half:].astype(F32)[:, :rows].reshape(tokens, 128)
+    target = (info[:, 0:1] * 256.0 + info[:, 1:2]).astype(jnp.int32) - v * shard
+    weight = info[:, 2:3]
     onehot = iota((tokens, shard), 1) == target
     logit_t = capped(lt[...])
     exp_t = jnp.exp(logit_t)
@@ -264,7 +278,7 @@
         hidden_ref[:, wide_s // 2 + q * cols:wide_s // 2 + (q + 1) * cols] = result[:, cols:]
 
     swap.wait_send()
-    for copy in meta_copies + stat_copies + back_copies:
+    for copy in stat_copies + back_copies:
         copy.wait_send()
     for c in range(CHUNKS):
         for d in range(far):
@@ -278,6 +292,11 @@
         for source_z in range(far):
             for step in range(1, near):
                 sideways(source_z * near + y, c, step).wait_send()
+
+
+def hand_on(loss_in, hidden_in, loss_ref, hidden_ref):
+    loss_ref[...] = loss_in[...]
+    hidden_ref[...] = hidden_in[...]
 
 
 def local(far, near, teacher_hidden, student_hidden, teacher_head, student_head, dest_slot, targets, token_grad):
@@ -288,7 +307,6 @@
     tokens = n * rows
     half = (wide_t + wide_s) // 2
     vmem = pl.BlockSpec(memory_space=pltpu.VMEM)
-    smem = pl.BlockSpec(memory_space=pltpu.SMEM)
     hbm = pl.BlockSpec(memory_space=pl.ANY)
     dma = pltpu.SemaphoreType.DMA
     loss, hidden = pl.pallas_call(
@@ -297,27 +315,29 @@
             jax.ShapeDtypeStruct((1, rows), F32),
             jax.ShapeDtypeStruct((rows, wide_s), BF16),
         ),
-        in_specs=[vmem, vmem, smem, smem, vmem, hbm, hbm],
+        in_specs=[hbm, hbm, hbm, hbm, vmem, hbm, hbm],
         out_specs=(vmem, vmem),
         scratch_shapes=[
+            pltpu.VMEM((rows, wide_t), BF16),
+            pltpu.VMEM((rows, wide_s), BF16),
+            pltpu.SMEM((rows,), jnp.int32),
+            pltpu.SMEM((rows,), jnp.int32),
             pltpu.VMEM((wide_t + wide_s, shard), BF16),
             pltpu.VMEM((2 * rows, wide_t // 2), BF16),
             pltpu.VMEM((2 * rows, wide_t // 2), BF16),
-            pltpu.VMEM((n, 2 * rows, half), BF16),
-            pltpu.VMEM((n, rows, 128), F32),
+            pltpu.VMEM((n, 2 * rows, half + 128), BF16),
             pltpu.VMEM((n, 8, tokens), F32),
             pltpu.VMEM((tokens, shard), F32),
             pltpu.VMEM((tokens, shard), F32),
             pltpu.VMEM((n, BACK, 2 * rows, wide_s // 2 // BACK), BF16),
             pltpu.VMEM((n - 1, BACK, 2 * rows, wide_s // 2 // BACK), BF16),
+            dma((4,)),
             dma((2,)),
             dma((2,)),
             dma((n, CHUNKS)),
             dma((far, CHUNKS)),
             dma((far, CHUNKS)),
             dma((near - 1, far, CHUNKS)),
-            dma((n - 1,)),
-            dma((n - 1,)),
             dma((n - 1,)),
             dma((n - 1,)),
             dma((n - 1, BACK)),
@@ -327,6 +347,12 @@
             collective_id=0, has_side_effects=True, vmem_limit_bytes=56 * 2**20
         ),
     )(teacher_hidden, student_hidden, dest_slot, targets, token_grad, teacher_head, student_head)
+    loss, hidden = pl.pallas_call(
+        hand_on,
+        out_shape=(jax.ShapeDtypeStruct((1, rows), F32), jax.ShapeDtypeStruct((rows, wide_s), BF16)),
+        in_specs=[vmem, vmem],
+        out_specs=(vmem, vmem),
+    )(loss, hidden)
     return loss.reshape(rows), hidden
 
 

time: 44.5 us -> 41.9 us (0.942)
  local copies, waits for them, and re-layouts: 2.56 us -> 0 us
    unnamed x2 -> x0, local copies, waits for them, and re-layouts: 2.56 us -> none
    pallas_call x1, Pallas kernels: 41.1 us -> 39.6 us  [local(): pl.pallas_call(functools.partial(kernel, far, near), out_shape=(jax.Shape...]
    pallas_call x0 -> x1, Pallas kernels: none -> 1.45 us  [local(): pl.pallas_call(hand_on, out_shape=(jax.ShapeDtypeStruct((1, rows), F32),...]
where the time goes in v2:
time: 41.9 us; the launch traced here: 41.7 us
  Pallas kernels  41.1 us (98%)
  between operations  0.64 us (2%)
    pallas_call x1, Pallas kernels, local(): pl.pallas_call(functools.partial(kernel, far, near), out_shape=(jax.Shape...  39.6 us
    pallas_call x1, Pallas kernels, local(): pl.pallas_call(hand_on, out_shape=(jax.ShapeDtypeStruct((1, rows), F32),...  1.45 us

profile of v2, /device:TPU:0, one launch (start us, length us, event | category | flops | bytes accessed | tf_op | source)
XLA Modules:
  0.0 41.7 jit_solution(8980725602386810217)
XLA Ops:
  0.6 39.6 %shard_map.86 = (f32[1,8]{1,0:T(1,128)}, bf16[8,3584]{1,0:T(8,128)(2,1)}) custom-call(bf16[8,4608]{1,0:T(8,128)(2,1)} %th_in.1, bf16[8,3584]{1,0:T(8,128)(2,1)} %sh_in.1, s32[8]{0:T(128)} %dest_in.1, s32[8]{0:T(128)} %target_in.1, bf16[8]{0:T(256)(128)(2,1)} %weight_ref.1, bf16[4608,640]{1,0:T(8,128)(2,1)} %thead_ref.1, bf16[3584,640]{1,0:T(8,128)(2,1)} %shead_ref.1), custom_call_target="tpu_custom_call" | custom-call | tf_op jit(solution)/shard_map/pallas_call | solution.py:312
  40.2 1.5 %shard_map.87 = (f32[1,8]{1,0:T(1,128)}, bf16[8,3584]{1,0:T(8,128)(2,1)}) custom-call(f32[1,8]{1,0:T(1,128)} %get-tuple-element.6.loss_in, bf16[8,3584]{1,0:T(8,128)(2,1)} %get-tuple-element.7.hidden_in), custom_call_target="tpu_custom_call" | custom-call | tf_op jit(solution)/shard_map/pallas_call | solution.py:350

commit v3 on v2

--- a/solution.py
+++ b/solution.py
@@ -8,7 +8,7 @@
 from jax.sharding import PartitionSpec as P
 
 soft_cap = 30.0
-CHUNKS = 2
+CROSS = 768
 BACK = 1
 F32 = jnp.float32
 BF16 = jnp.bfloat16
@@ -50,8 +50,16 @@
     n = far * near
     rows, wide_t = th_ref.shape
     wide_s = sh_ref.shape[1]
-    half = (wide_t + wide_s) // 2
-    chunk = half // CHUNKS
+    half_s, half_t = wide_s // 2, wide_t // 2
+    gap = half_s + 128
+    kept_t = half_t - CROSS
+    chunks = [
+        (0, gap, half_s, ls, (wide_t, wide_t + half_s), False),
+        (gap, kept_t, kept_t, lt, (0, half_t), False),
+    ]
+    if CROSS:
+        chunks.append((gap + kept_t, CROSS, CROSS, lt, (kept_t, half_t + kept_t), True))
+    count = len(chunks)
     shard = heads.shape[1]
     tokens = n * rows
     v = lax.axis_index("vocab")
@@ -125,21 +133,19 @@
             copies[-1].start()
         return copies
 
-    swap.wait_recv()
-    moved = swap_in[...].astype(F32)
-    aligned = kept + jnp.concatenate([moved[:rows], moved[rows:]], axis=1)
-    own = stacked(jnp.concatenate([aligned, sh_ref[...].astype(F32)], axis=1))
-    blocks[v, :, :half] = own.astype(BF16)
-    blocks[v, :, half:] = jnp.concatenate([own_meta, jnp.zeros_like(own_meta)], axis=0).astype(BF16)
+    student = stacked(sh_ref[...].astype(F32))
+    blocks[v, :, :half_s] = student.astype(BF16)
+    blocks[v, :, half_s:gap] = jnp.concatenate(
+        [own_meta, jnp.zeros_like(own_meta)], axis=0
+    ).astype(BF16)
 
     def piece(source, c):
-        return blocks.at[source, :, pl.ds(c * chunk, chunk + 128 if c == CHUNKS - 1 else chunk)]
+        return blocks.at[source, :, pl.ds(chunks[c][0], chunks[c][1])]
 
     def vertical(source, c, up):
-        source_z = lax.div(source, near)
         sems = up_sem if up else down_sem
         return pltpu.make_async_remote_copy(
-            piece(source, c), piece(source, c), sems.at[source_z, c], arrive.at[source, c],
+            piece(source, c), piece(source, c), sems.at[source, c], arrive.at[source, c],
             device_id={"vocab": v + near if up else v - near},
         )
 
@@ -151,7 +157,7 @@
             device_id={"vocab": z * near + lax.rem(y + step, near)},
         )
 
-    def spread(source, c, up, down):
+    def spread(source, c, up, down, across):
         if up:
             @pl.when(z < far - 1)
             def _():
@@ -160,44 +166,57 @@
             @pl.when(z > 0)
             def _():
                 vertical(source, c, False).start()
-        for step in range(1, near):
-            sideways(source, c, step).start()
+        if across:
+            for step in range(1, near):
+                sideways(source, c, step).start()
 
     def product(c):
-        both = blocks[:, :, c * chunk:(c + 1) * chunk].astype(F32)
+        start, _, width, out, tops, _ = chunks[c]
+        both = blocks[:, :, start:start + width].astype(F32)
+        value = 0.0
         for part in range(2):
-            x = both[:, part * rows:(part + 1) * rows].reshape(tokens, chunk).astype(BF16)
-            first = part * half + c * chunk
-            for out, begin, end in ((lt, 0, wide_t), (ls, wide_t, wide_t + wide_s)):
-                low, high = max(first, begin), min(first + chunk, end)
-                if low < high:
-                    out[...] += jnp.dot(
-                        x[:, low - first:high - first], heads[low:high, :],
-                        preferred_element_type=F32,
-                    )
-
-    lt[...] = jnp.zeros_like(lt)
-    ls[...] = jnp.zeros_like(ls)
-    spread(v, 0, True, True)
-    for t in range(CHUNKS + far):
-        if t == 0:
-            for c in range(1, CHUNKS):
-                spread(v, c, True, True)
+            x = both[:, part * rows:(part + 1) * rows].reshape(tokens, width).astype(BF16)
+            value += jnp.dot(
+                x, heads[tops[part]:tops[part] + width, :], preferred_element_type=F32
+            )
+        if c == 2:
+            value += out[...]
+        out[...] = value
+
+    def places(c):
+        return [lax.rem(y + step, near) for step in range(near if chunks[c][5] else 1)]
+
+    spread(v, 0, True, True, True)
+    swap.wait_recv()
+    aligned = stacked(kept) + swap_in[...].astype(F32)
+    blocks[v, :, gap:] = aligned.astype(BF16)
+    for c in range(1, count):
+        spread(v, c, True, True, True)
+    for t in range(count + far):
+        if t >= 1 and t < count and chunks[t][5]:
+            for step in range(1, near):
+                beside = z * near + lax.rem(y + step, near)
+                sideways(beside, t, step).wait_recv()
+                spread(beside, t, True, True, False)
         for d in range(1, far):
             c = t - d
-            if 0 <= c < CHUNKS:
+            if 0 <= c < count:
                 @pl.when(z >= d)
                 def _():
-                    vertical(v - d * near, c, True).wait_recv()
-                    spread(v - d * near, c, True, False)
+                    for at in places(c):
+                        source = (z - d) * near + at
+                        vertical(source, c, True).wait_recv()
+                        spread(source, c, True, False, not chunks[c][5])
 
                 @pl.when(z + d < far)
                 def _():
-                    vertical(v + d * near, c, False).wait_recv()
-                    spread(v + d * near, c, False, True)
+                    for at in places(c):
+                        source = (z + d) * near + at
+                        vertical(source, c, False).wait_recv()
+                        spread(source, c, False, True, not chunks[c][5])
         c = t - far
         if c >= 0:
-            for step in range(1, near):
+            for step in range(1, 1 if chunks[c][5] else near):
                 for source_z in range(far):
                     source = source_z * near + lax.rem(y + step, near)
                     sideways(source, c, step).wait_recv()
@@ -206,7 +225,7 @@
                     load.wait()
             product(c)
 
-    info = blocks[:, :, half:].astype(F32)[:, :rows].reshape(tokens, 128)
+    info = blocks[:, :, half_s:gap].astype(F32)[:, :rows].reshape(tokens, 128)
     target = (info[:, 0:1] * 256.0 + info[:, 1:2]).astype(jnp.int32) - v * shard
     weight = info[:, 2:3]
     onehot = iota((tokens, shard), 1) == target
@@ -280,18 +299,24 @@
     swap.wait_send()
     for copy in stat_copies + back_copies:
         copy.wait_send()
-    for c in range(CHUNKS):
+    for c in range(count):
         for d in range(far):
             @pl.when((z >= d) & (z < far - 1))
             def _():
-                vertical(v - d * near, c, True).wait_send()
+                for at in places(c):
+                    vertical((z - d) * near + at, c, True).wait_send()
 
             @pl.when((z + d < far) & (z > 0))
             def _():
-                vertical(v + d * near, c, False).wait_send()
-        for source_z in range(far):
+                for at in places(c):
+                    vertical((z + d) * near + at, c, False).wait_send()
+        if chunks[c][5]:
             for step in range(1, near):
-                sideways(source_z * near + y, c, step).wait_send()
+                sideways(v, c, step).wait_send()
+        else:
+            for source_z in range(far):
+                for step in range(1, near):
+                    sideways(source_z * near + y, c, step).wait_send()
 
 
 def hand_on(loss_in, hidden_in, loss_ref, hidden_ref):
@@ -334,10 +359,10 @@
             dma((4,)),
             dma((2,)),
             dma((2,)),
-            dma((n, CHUNKS)),
-            dma((far, CHUNKS)),
-            dma((far, CHUNKS)),
-            dma((near - 1, far, CHUNKS)),
+            dma((n, 3)),
+            dma((n, 3)),
+            dma((n, 3)),
+            dma((near - 1, far, 3)),
             dma((n - 1,)),
             dma((n - 1,)),
             dma((n - 1, BACK)),

time: 41.9 us -> 39.8 us (0.950)
  Pallas kernels: 41.1 us -> 39 us
    pallas_call x1, Pallas kernels: 39.6 us -> 37.6 us  [local(): pl.pallas_call(functools.partial(kernel, far, near), out_shape=(jax.Shape...]
where the time goes in v3:
time: 39.8 us; the launch traced here: 39.7 us
  Pallas kernels  39 us (98%)
  between operations  0.64 us (2%)
    pallas_call x1, Pallas kernels, local(): pl.pallas_call(functools.partial(kernel, far, near), out_shape=(jax.Shape...  37.6 us
    pallas_call x1, Pallas kernels, local(): pl.pallas_call(hand_on, out_shape=(jax.ShapeDtypeStruct((1, rows), F32),...  1.45 us

profile of v3, /device:TPU:0, one launch (start us, length us, event | category | flops | bytes accessed | tf_op | source)
XLA Modules:
  0.0 39.7 jit_solution(13430577550293065676)
XLA Ops:
  0.6 37.6 %shard_map.86 = (f32[1,8]{1,0:T(1,128)}, bf16[8,3584]{1,0:T(8,128)(2,1)}) custom-call(bf16[8,4608]{1,0:T(8,128)(2,1)} %th_in.1, bf16[8,3584]{1,0:T(8,128)(2,1)} %sh_in.1, s32[8]{0:T(128)} %dest_in.1, s32[8]{0:T(128)} %target_in.1, bf16[8]{0:T(256)(128)(2,1)} %weight_ref.1, bf16[4608,640]{1,0:T(8,128)(2,1)} %thead_ref.1, bf16[3584,640]{1,0:T(8,128)(2,1)} %shead_ref.1), custom_call_target="tpu_custom_call" | custom-call | tf_op jit(solution)/shard_map/pallas_call | solution.py:337
  38.2 1.5 %shard_map.87 = (f32[1,8]{1,0:T(1,128)}, bf16[8,3584]{1,0:T(8,128)(2,1)}) custom-call(f32[1,8]{1,0:T(1,128)} %get-tuple-element.6.loss_in, bf16[8,3584]{1,0:T(8,128)(2,1)} %get-tuple-element.7.hidden_in), custom_call_target="tpu_custom_call" | custom-call | tf_op jit(solution)/shard_map/pallas_call | solution.py:375

commit v4 on v3

--- a/solution.py
+++ b/solution.py
@@ -121,9 +121,11 @@
     )
     swap.start()
 
+    order = list(range(1, n))
+
     def to_all(src, dst, sends, recvs):
         copies = []
-        for step in range(1, n):
+        for step in order:
             copies.append(
                 pltpu.make_async_remote_copy(
                     src, dst, sends.at[step - 1], recvs.at[step - 1],
@@ -224,20 +226,24 @@
                 for load in loads:
                     load.wait()
             product(c)
-
-    info = blocks[:, :, half_s:gap].astype(F32)[:, :rows].reshape(tokens, 128)
-    target = (info[:, 0:1] * 256.0 + info[:, 1:2]).astype(jnp.int32) - v * shard
-    weight = info[:, 2:3]
-    onehot = iota((tokens, shard), 1) == target
+            if c == 0:
+                info = blocks[:, :, half_s:gap].astype(F32)[:, :rows].reshape(tokens, 128)
+                target = (info[:, 0:1] * 256.0 + info[:, 1:2]).astype(jnp.int32) - v * shard
+                weight = info[:, 2:3]
+                onehot = iota((tokens, shard), 1) == target
+                logit_s = capped(ls[...])
+                exp_s = jnp.exp(logit_s)
+                sum_s = jnp.sum(exp_s, axis=1, keepdims=True)
+                sum_hit = jnp.sum(jnp.where(onehot, logit_s, 0.0), axis=1, keepdims=True)
+                slope = 1.0 - (logit_s / soft_cap) * (logit_s / soft_cap)
+
     logit_t = capped(lt[...])
     exp_t = jnp.exp(logit_t)
-    logit_s = capped(ls[...])
-    exp_s = jnp.exp(logit_s)
     sums = (
         jnp.sum(exp_t, axis=1, keepdims=True),
         jnp.sum(exp_t * (logit_t - logit_s), axis=1, keepdims=True),
-        jnp.sum(exp_s, axis=1, keepdims=True),
-        jnp.sum(jnp.where(onehot, logit_s, 0.0), axis=1, keepdims=True),
+        sum_s,
+        sum_hit,
     )
     stat_row = iota((8, tokens), 0)
     mine = jnp.zeros((8, tokens), F32)
@@ -245,17 +251,14 @@
         mine = jnp.where(stat_row == k, to_row(column), mine)
     stats[v] = mine
     stat_copies = to_all(stats.at[v], stats.at[v], stat_send, stat_recv)
-    slope = 1.0 - (logit_s / soft_cap) * (logit_s / soft_cap)
+    scale = weight * slope
+    grad_s, grad_t, grad_hit = 2.0 * scale * exp_s, scale * exp_t, jnp.where(onehot, scale, 0.0)
     for copy in stat_copies:
         copy.wait_recv()
     total = jnp.sum(stats[...], axis=0)
     norm_t, cross, norm_s, hit = (total[k:k + 1] for k in range(4))
     zt, zs = to_column(norm_t), to_column(norm_s)
-    grad = (
-        weight
-        * (exp_s * (2.0 / zs) - exp_t * (1.0 / zt) - jnp.where(onehot, 1.0, 0.0))
-        * slope
-    ).astype(BF16)
+    grad = (grad_s * (1.0 / zs) - grad_t * (1.0 / zt) - grad_hit).astype(BF16)
 
     cols = wide_s // 2 // BACK
 
@@ -270,7 +273,7 @@
     for q in range(BACK):
         joined = jnp.concatenate([backed(q, 0), backed(q, 1)], axis=1)
         back_out[:, q] = joined.astype(BF16)
-        for step in range(1, n):
+        for step in order:
             there = lax.rem(v + step, n)
             back_copies.append(
                 pltpu.make_async_remote_copy(
@@ -288,7 +291,7 @@
     k = 0
     for q in range(BACK):
         result = back_out[v, q].astype(F32)
-        for step in range(1, n):
+        for step in order:
             back_copies[k].wait_recv()
             k += 1
             result += back_in[step - 1, q].astype(F32)

time: 39.8 us -> 39.8 us (level)
  no operation moved by 1% of the time
where the time goes in v4:
time: 39.8 us; the launch traced here: 39.7 us
  Pallas kernels  39 us (98%)
  between operations  0.64 us (2%)
    pallas_call x1, Pallas kernels, local(): pl.pallas_call(functools.partial(kernel, far, near), out_shape=(jax.Shape...  37.6 us
    pallas_call x1, Pallas kernels, local(): pl.pallas_call(hand_on, out_shape=(jax.ShapeDtypeStruct((1, rows), F32),...  1.45 us

profile of v4, /device:TPU:0, one launch (start us, length us, event | category | flops | bytes accessed | tf_op | source)
XLA Modules:
  0.0 39.7 jit_solution(7227610374316911928)
XLA Ops:
  0.6 37.6 %shard_map.86 = (f32[1,8]{1,0:T(1,128)}, bf16[8,3584]{1,0:T(8,128)(2,1)}) custom-call(bf16[8,4608]{1,0:T(8,128)(2,1)} %th_in.1, bf16[8,3584]{1,0:T(8,128)(2,1)} %sh_in.1, s32[8]{0:T(128)} %dest_in.1, s32[8]{0:T(128)} %target_in.1, bf16[8]{0:T(256)(128)(2,1)} %weight_ref.1, bf16[4608,640]{1,0:T(8,128)(2,1)} %thead_ref.1, bf16[3584,640]{1,0:T(8,128)(2,1)} %shead_ref.1), custom_call_target="tpu_custom_call" | custom-call | tf_op jit(solution)/shard_map/pallas_call | solution.py:340
  38.2 1.5 %shard_map.87 = (f32[1,8]{1,0:T(1,128)}, bf16[8,3584]{1,0:T(8,128)(2,1)}) custom-call(f32[1,8]{1,0:T(1,128)} %get-tuple-element.6.loss_in, bf16[8,3584]{1,0:T(8,128)(2,1)} %get-tuple-element.7.hidden_in), custom_call_target="tpu_custom_call" | custom-call | tf_op jit(solution)/shard_map/pallas_call | solution.py:378
